TPU v7x, 512 devices: a whole 4x4x16 slice. The times are simulated.
512 devices in a mesh: tri: 64 (over y, z), sub: 8 (over x, core).
Axes of the slice: x: 4, y: 4, z: 16, core: 2. Of those that a mesh axis runs over, the one named last changes fastest.
Arguments:
- stored_tiles: float32 [64, 10, 512, 512], P('tri', None, 'sub'), may hold values from -190 to 190, as said below
- cell_owner: int32 [64], replicated, may hold values from 0 to 63, as said below
Outputs:
- updated: float32 [64, 10, 512, 512], P('tri', None, 'sub')
Inputs may be any that keep to these rules, and one draw needn't show every extreme that they name: `cell_owner`: a permutation of the indices of tri. `stored_tiles`: every tile whose row and column blocks are equal is skew-symmetric, every pivot met is invertible, and slots that hold no tile are zero.
All inputs are finite; a program needn't handle non-finite values.
Results may differ from a plain program's by a relative error of at most 0.00035.
Values may be sent and summed in bfloat16 or wider, within the bound.
A program may use at most 64 MiB of HBM per device.

v0:
```python
import math
import jax
import jax.numpy as jnp
import numpy as np
from jax import lax
from jax.sharding import Mesh
from jax.sharding import PartitionSpec as P

NB = 32
TRI = ("tri_0", "tri_1")


def in_order(tiles, dim):
    tiles = jnp.moveaxis(tiles, 0, dim)
    dims = tiles.shape
    return tiles.reshape(*dims[:dim], dims[dim] * dims[dim + 1], *dims[dim + 2 :])


def gather_in_order(x, axes, turns):
    tiles = x[None]
    for k in turns:
        tiles = lax.all_gather(tiles, axes[k], axis=0, tiled=True)
    block = [lax.axis_size(axes[k]) for k in reversed(turns)]
    tiles = tiles.reshape(*block, *x.shape)
    turned = sorted(range(len(turns)), key=lambda place: turns[len(turns) - 1 - place])
    return tiles.transpose(*turned, *range(len(turns), tiles.ndim)).reshape(-1, *x.shape)


def gather_axes(x, axes, turns, dim):
    return in_order(gather_in_order(x, axes, turns), dim)


def layout(groups, per_group):
    half_group = per_group // 2
    slot_count = per_group * (per_group + 1) // 2
    row_table = np.full((groups * groups, slot_count), -1, np.int32)
    col_table = np.full((groups * groups, slot_count), -1, np.int32)
    for first_group in range(groups):
        for second_group in range(groups):
            cell_index = first_group * groups + second_group
            for inner_row in range(per_group):
                if first_group == second_group:
                    for inner_column in range(inner_row + 1):
                        slot_index = inner_row * (inner_row + 1) // 2 + inner_column
                        row_table[cell_index, slot_index] = first_group * per_group + inner_row
                        col_table[cell_index, slot_index] = first_group * per_group + inner_column
                else:
                    for inner_column in range(half_group):
                        slot_index = inner_row * half_group + inner_column
                        if first_group > second_group:
                            row_table[cell_index, slot_index] = first_group * per_group + inner_row
                            col_table[cell_index, slot_index] = (
                                second_group * per_group + inner_column
                            )
                        else:
                            row_table[cell_index, slot_index] = second_group * per_group + inner_row
                            col_table[cell_index, slot_index] = (
                                first_group * per_group + half_group + inner_column
                            )
    return (row_table, col_table)


def shards(stored_tiles, cell_owner):
    tri_count = lax.axis_size(TRI)
    groups = math.isqrt(tri_count)
    per_group = NB // groups
    half_group = per_group // 2
    strip_rows = stored_tiles.shape[2]
    block_order = stored_tiles.shape[3]
    row_table, col_table = layout(groups, per_group)
    position = lax.axis_index(TRI)
    my_cell = jnp.sum(jnp.where(cell_owner == position, jnp.arange(tri_count, dtype=jnp.int32), 0))
    cell_down = my_cell // groups
    cell_across = my_cell % groups
    row_group = jnp.maximum(cell_down, cell_across)
    col_group = jnp.minimum(cell_down, cell_across)
    my_rows = jnp.asarray(row_table)[my_cell]
    my_cols = jnp.asarray(col_table)[my_cell]
    row_local = jnp.clip(my_rows - row_group * per_group, 0, per_group - 1)
    col_local = jnp.clip(my_cols - col_group * per_group, 0, per_group - 1)
    holders = cell_owner[jnp.arange(groups) * groups]
    highest = lax.Precision.HIGHEST
    current = stored_tiles[0]
    lower_slots = np.array([member * half_group for member in range(per_group)], np.int32)
    first_slots = np.array(
        [member * (member + 1) // 2 if member > 0 else 0 for member in range(per_group)], np.int32
    )
    keep_first = np.array([1.0 if member > 0 else 0.0 for member in range(per_group)], np.float32)
    from_lower = current[lower_slots]
    from_first = current[first_slots] * keep_first[:, None, None]
    holder_part = jnp.where(cell_down > 0, from_lower, from_first)
    holder_part = jnp.where(cell_across == 0, holder_part, 0.0).astype(jnp.bfloat16)
    pivot_slot = 0 // 2
    pivot_part = jnp.where(my_cell == 0, current[pivot_slot], 0.0)
    piece_size = holder_part.size // tri_count
    spread_panel = lax.all_to_all(
        holder_part.reshape(tri_count, piece_size), TRI, split_axis=0, concat_axis=0, tiled=True
    )
    spread_pivot = lax.all_to_all(
        pivot_part.astype(jnp.bfloat16), TRI, split_axis=0, concat_axis=0, tiled=True
    ).astype(pivot_part.dtype)
    picked_panel = spread_panel[holders][:, None, :]
    picked_pivot = spread_pivot[holders[0]][None, :]
    whole_panel = gather_axes(picked_panel, TRI, (0, 1), 1)
    whole_pivot = gather_axes(picked_pivot.astype(jnp.bfloat16), TRI, (0, 1), 0).astype(
        picked_pivot.dtype
    )
    panels = whole_panel.reshape(groups, per_group, strip_rows, block_order)
    own_strips = panels[row_group]
    other_strips = panels[col_group]
    pivot_block = lax.all_gather(
        whole_pivot.astype(jnp.bfloat16), "sub", axis=0, tiled=True
    ).astype(whole_pivot.dtype)
    partner = lax.all_gather(other_strips, "sub", axis=1, tiled=True)
    gram_matrix = jnp.dot(pivot_block.T, pivot_block, precision=highest)
    factor = jnp.linalg.cholesky(gram_matrix)
    inverse = jax.scipy.linalg.cho_solve((factor, True), pivot_block.T)
    scaled = jnp.einsum(
        "irk,kc->irc", own_strips.astype(jnp.float32), inverse, precision=highest
    ).astype(jnp.bfloat16)
    left_slots = scaled[row_local]
    right_slots = partner[col_local]
    update = jnp.einsum("qrk,qck->qrc", left_slots, right_slots, preferred_element_type=jnp.float32)
    live_slots = (my_rows > 0) & (my_cols > 0)
    current = current + jnp.where(live_slots[:, None, None], update, 0.0)
    return current[None]


def solution(mesh):
    torus = Mesh(mesh.devices.reshape(4, 16, mesh.shape["sub"]), ("tri_0", "tri_1", "sub"))
    return jax.shard_map(
        shards,
        mesh=torus,
        in_specs=(P(TRI, None, "sub", None), P()),
        out_specs=P(TRI, None, "sub", None),
        check_vma=False,
    )
```

profile of v0, /device:TPU:1, one launch (start us, length us, event | category | flops | bytes accessed | tf_op | source)
XLA Modules:
  0.0 323.7 jit_solution(5538113034983923474)
XLA Ops:
  11.3 19.3 %all-to-all-start.1 = ((bf16[64,2,256]{2,1,0:T(2,128)(2,1)}), bf16[64,2,256]{2,1,0:T(2,128)(2,1)S(1)}, u32[]{:S(2)}, u32[]{:S(2)}) async-start(bf16[64,2,256]{2,1,0:T(2,128)(2,1)} %reshape.305), calls=%async_computation.1 | async-start | bytes 131072 | tf_op jit(solution)/shard_map/all_to_all | solution.py:99
  43.2 2.1 reduce.26
  46.2 14.6 %all-to-all-start = ((bf16[64,2,1024]{2,1,0:T(2,128)(2,1)}), bf16[64,2,1024]{2,1,0:T(2,128)(2,1)S(1)}, u32[]{:S(2)}, u32[]{:S(2)}) async-start(bf16[64,2,1024]{2,1,0:T(2,128)(2,1)} %reshape.307), calls=%async_computation | async-start | bytes 524288 | tf_op jit(solution)/shard_map/all_to_all | solution.py:96
  60.9 8.8 %all_gather.20 = bf16[4,1,512]{2,1,0:T(2,128)(2,1)S(1)} all-gather(bf16[1,1,512]{2,1,0:T(2,128)(2,1)S(1)} %fusion.54), channel_id=1, replica_groups=mesh['tri_0'=4,'tri_1'=16,'sub'=8] {'tri_0'}, dimensions={0}, use_global_device_ids=true | all-gather | bytes 5120 | tf_op jit(solution)/shard_map/all_gather | solution.py:22
  69.7 23.8 %all_gather.21 = bf16[64,1,512]{2,1,0:T(2,128)(2,1)S(1)} all-gather(bf16[4,1,512]{2,1,0:T(2,128)(2,1)S(1)} %all_gather.20), channel_id=1, replica_groups=mesh['tri_0'=4,'tri_1'=16,'sub'=8] {'tri_1'}, dimensions={0}, use_global_device_ids=true | all-gather | bytes 69632 | tf_op jit(solution)/shard_map/all_gather | solution.py:22
  93.9 23.9 %all_gather.22 = bf16[512,512]{1,0:T(8,128)(2,1)S(1)} all-gather(bf16[64,512]{1,0:T(8,128)(2,1)S(1)} %bitcast.120), channel_id=1, replica_groups=mesh['tri_0'=4,'tri_1'=16,'sub'=8] {'sub'}, dimensions={0}, use_global_device_ids=true | all-gather | bytes 589824 | tf_op jit(solution)/shard_map/all_gather | solution.py:111
  119.9 11.7 %cholesky.104 = f32[128,128]{1,0:T(8,128)S(1)} custom-call(f32[128,128]{1,0:T(8,128)S(1)} %cholesky.266), custom_call_target="Cholesky" | custom-call | tf_op jit(solution)/shard_map/jit(cholesky)/cholesky | solution.py:116
  131.6 9.8 %custom-call.34 = f32[1,128,128]{1,2,0:T(8,128)S(1)} custom-call(f32[1,128,128]{2,1,0:T(8,128)S(1)} %get-tuple-element.32), custom_call_target="InvertDiagBlocksLowerTriangular" | custom-call | tf_op jit(solution)/shard_map/jit(cholesky)/cholesky | solution.py:116
  142.6 9.8 %all-gather = bf16[32,2048]{1,0:T(8,128)(2,1)} all-gather(bf16[8,2048]{1,0:T(8,128)(2,1)S(1)} %gather_fusion.3), channel_id=2, replica_groups=mesh['tri_0'=4,'tri_1'=16,'sub'=8] {'tri_0'}, dimensions={0}, use_global_device_ids=true | all-gather | bytes 163840 | tf_op jit(solution)/shard_map/all_gather | solution.py:22
  154.3 11.7 %cholesky.217 = f32[128,128]{1,0:T(8,128)S(1)} custom-call(f32[128,128]{1,0:T(8,128)S(1)} %cholesky.270), custom_call_target="Cholesky" | custom-call | tf_op jit(solution)/shard_map/jit(cholesky)/cholesky | solution.py:116
  166.1 9.8 %custom-call.35 = f32[1,128,128]{1,2,0:T(8,128)S(1)} custom-call(f32[1,128,128]{2,1,0:T(8,128)S(1)} %get-tuple-element.29), custom_call_target="InvertDiagBlocksLowerTriangular" | custom-call | tf_op jit(solution)/shard_map/jit(cholesky)/cholesky | solution.py:116
  176.6 11.7 %cholesky.238 = f32[128,128]{1,0:T(8,128)S(1)} custom-call(f32[128,128]{1,0:T(8,128)S(1)} %cholesky.275), custom_call_target="Cholesky" | custom-call | tf_op jit(solution)/shard_map/jit(cholesky)/cholesky | solution.py:116
  188.3 10.0 %custom-call.36 = f32[1,128,128]{1,2,0:T(8,128)S(1)} custom-call(f32[1,128,128]{2,1,0:T(8,128)S(1)} %get-tuple-element.26), custom_call_target="InvertDiagBlocksLowerTriangular" | custom-call | tf_op jit(solution)/shard_map/jit(cholesky)/cholesky | solution.py:116
  198.9 11.7 %cholesky.255 = f32[128,128]{1,0:T(8,128)S(1)} custom-call(f32[128,128]{1,0:T(8,128)S(1)} %convolution_subtract_fusion.8), custom_call_target="Cholesky" | custom-call | tf_op jit(solution)/shard_map/jit(cholesky)/cholesky | solution.py:116
  215.7 10.8 %while.1 = (s32[]{:T(128)}, f32[512,512]{1,0:T(8,128)S(1)}, s32[4,2]{0,1:T(2,128)S(1)}, f32[4,128,128]{2,1,0:T(8,128)}, s32[]{:T(128)}) while((s32[]{:T(128)}, f32[512,512]{1,0:T(8,128)S(1)}, s32[4,2]{0,1:T(2,128)S(1)}, f32[4,128,128]{2,1,0:T(8,128)}, s32[]{:T(128)}) %tuple.27), condition=%wide.while_cond, body=%wide.while_body.sunk | while | flops 2 | bytes 132705 | solution.py:117
  216.4 2.0 bitcast_dynamic-update-slice_fusion.2
  219.1 2.0 bitcast_dynamic-update-slice_fusion.2
  221.8 2.0 bitcast_dynamic-update-slice_fusion.2
  224.5 2.0 bitcast_dynamic-update-slice_fusion.2
  226.5 40.1 %custom-call.37 = f32[4,128,128]{1,2,0:T(8,128)S(1)} custom-call(f32[4,128,128]{2,1,0:T(8,128)} %get-tuple-element.12), custom_call_target="InvertDiagBlocksLowerTriangular" | custom-call | tf_op jit(solution)/shard_map/jit(_cho_solve)/triangular_solve | solution.py:117
  269.6 2.6 reshape_reshape.6
  284.3 21.5 %all-gather.7.cloned.1.call-done = bf16[1,4,512,512]{3,2,1,0:T(8,128)(2,1)} async-done(((bf16[1,4,64,512]{3,2,1,0:T(8,128)(2,1)}), bf16[1,4,512,512]{3,2,1,0:T(8,128)(2,1)}) %all-gather.7.cloned.1.call-update) | async-done | bytes 2097168 | tf_op jit(solution)/shard_map/all_gather | solution.py:114
  305.8 5.5 %gather_fusion.5 = bf16[10,512,512]{2,1,0:T(8,128)(2,1)} fusion(bf16[4,512,512]{2,1,0:T(8,128)(2,1)} %bitcast.112, s32[1024]{0:T(1024)S(1)} %pad_clamp_fusion), kind=kCustom, calls=%fused_computation.5 | custom fusion | bytes 10485800 | tf_op jit(solution)/shard_map/gather | solution.py:122
  311.4 5.2 %fusion.1 = f32[1,10,64,512]{3,2,1,0:T(8,128)} fusion(bf16[10,64,512]{2,1,0:T(8,128)(2,1)S(1)} %gather_fusion.4, bf16[10,512,512]{2,1,0:T(8,128)(2,1)} %gather_fusion.5, pred[10]{0:T(512)(128)(4,1)S(1)} %and_bitcast_fusion, f32[1,10,64,512]{3,2,1,0:T(8,128)S(1)} %copy-done), kind=kOutput, calls=%fused_computation.10 | convolution fusion | flops 336199680 | bytes 8519690 | tf_op jit(solution)/shard_map/qrk,qck->qrc/dot_general | solution.py:123
  (99 shorter events, 39.9 us)
Async XLA Ops:
  6.5 35.5 %copy-start.3 = (f32[4]{0:T(128)S(1)}, f32[4]{0:T(128)}, u32[]{:S(2)}) copy-start(f32[4]{0:T(128)} %constant.245) | copy-start | bytes 52
  11.3 34.9 %all-to-all-start.1 = ((bf16[64,2,256]{2,1,0:T(2,128)(2,1)}), bf16[64,2,256]{2,1,0:T(2,128)(2,1)S(1)}, u32[]{:S(2)}, u32[]{:S(2)}) async-start(bf16[64,2,256]{2,1,0:T(2,128)(2,1)} %reshape.305), calls=%async_computation.1 | async-start | bytes 131072 | tf_op jit(solution)/shard_map/all_to_all | solution.py:99
  46.2 95.4 %all-to-all-start = ((bf16[64,2,1024]{2,1,0:T(2,128)(2,1)}), bf16[64,2,1024]{2,1,0:T(2,128)(2,1)S(1)}, u32[]{:S(2)}, u32[]{:S(2)}) async-start(bf16[64,2,1024]{2,1,0:T(2,128)(2,1)} %reshape.307), calls=%async_computation | async-start | bytes 524288 | tf_op jit(solution)/shard_map/all_to_all | solution.py:96
  60.8 205.9 %all-gather.5.cloned.1.call-start = ((), (), s32[]{:S(2)}) async-start(), calls=%async_computation.2 | async-start | bytes 2228224 | tf_op jit(solution)/shard_map/all_gather | solution.py:22
  118.9 1.0 copy-start.1
  119.9 32.8 %copy-start.2 = (f32[512,512]{1,0:T(8,128)S(1)}, f32[512,512]{1,0:T(8,128)}, u32[]{:S(2)}) copy-start(f32[512,512]{1,0:T(8,128)} %copy-done.1) | copy-start | bytes 3145732
  152.4 153.4 %all-gather.7.cloned.1.call-start = ((), (), s32[]{:S(2)}) async-start(), calls=%async_computation.3 | async-start | bytes 2359296 | tf_op jit(solution)/shard_map/all_gather | solution.py:114
  305.8 5.6 %copy-start = (f32[1,10,64,512]{3,2,1,0:T(8,128)S(1)}, f32[1,10,64,512]{3,2,1,0:T(8,128)}, u32[]{:S(2)}) copy-start(f32[1,10,64,512]{3,2,1,0:T(8,128)} %param.9) | copy-start | bytes 3932164
Sparse Core Ops, SparseCore 0:
  152.6 63.2 all-gather.4
  274.0 31.7 all-gather.6
where the time goes:
time: 329 us; the launch traced here: 324 us
  other arithmetic  129 us (39%)
  blocking collectives  66.3 us (20%)
  local copies, waits for them, and re-layouts  34.9 us (11%)
  starting transfers between devices  34.1 us (10%)
  between operations  21.9 us (7%)
  waiting for transfers between devices  21.6 us (7%)
  matrix products  16.1 us (5%)
    another operation x14, other arithmetic, shards(): factor = jnp.linalg.cholesky(gram_matrix)  78.8 us
    all_gather x3, blocking collectives, gather_in_order(): tiles = lax.all_gather(tiles, axes[k], axis=0, tiled=True)  42.5 us
    another operation x3, other arithmetic, shards(): inverse = jax.scipy.linalg.cho_solve((factor, True), pivot_block.T)  40.3 us
    all_gather x1, blocking collectives, shards(): lax.all_gather(whole_pivot.astype(jnp.bfloat16), 'sub', axis=0, tiled=True)  23.9 us
    all_gather x1, waiting for transfers between devices, shards(): partner = lax.all_gather(other_strips, 'sub', axis=1, tiled=True)  21.5 us
    all_to_all x1, starting transfers between devices, shards(): lax.all_to_all(pivot_part.astype(jnp.bfloat16), TRI, split_axis=0, concat...  19.3 us
    all_to_all x1, starting transfers between devices, shards(): lax.all_to_all(holder_part.reshape(tri_count, piece_size), TRI, split_axi...  14.6 us
    another operation x12, local copies, waits for them, and re-layouts  10.8 us
  transfers between devices with their start and end apart: 4, of which 1 were waited for; matrix products, arithmetic and copies ran while one was open for 48% of the time, Pallas kernels for 0%

commit v1 on v0

--- a/solution.py
+++ b/solution.py
@@ -111,7 +111,8 @@
     pivot_block = lax.all_gather(
         whole_pivot.astype(jnp.bfloat16), "sub", axis=0, tiled=True
     ).astype(whole_pivot.dtype)
-    partner = lax.all_gather(other_strips, "sub", axis=1, tiled=True)
+    outgoing = jnp.stack([other_strips] * lax.axis_size("sub"))
+    partner = jnp.concatenate(lax.all_to_all(outgoing, "sub", 0, 0), axis=1)
     gram_matrix = jnp.dot(pivot_block.T, pivot_block, precision=highest)
     factor = jnp.linalg.cholesky(gram_matrix)
     inverse = jax.scipy.linalg.cho_solve((factor, True), pivot_block.T)

time: 329 us -> 340 us (1.033)
  starting transfers between devices: 34.1 us -> 41.6 us
  matrix products: 16.1 us -> 19.7 us
    all_gather x1 -> x0, waiting for transfers between devices: 21.5 us -> none  [shards(): partner = lax.all_gather(other_strips, 'sub', axis=1, tiled=True)]
    all_to_all x0 -> x1, waiting for transfers between devices: none -> 19.7 us  [shards(): partner = jnp.concatenate(lax.all_to_all(outgoing, 'sub', 0, 0), axis=1)]
    all_to_all x0 -> x1, starting transfers between devices: none -> 7.7 us  [shards(): partner = jnp.concatenate(lax.all_to_all(outgoing, 'sub', 0, 0), axis=1)]
    another operation x6, matrix products: 1.86 us -> 5.46 us  [shards(): factor = jnp.linalg.cholesky(gram_matrix)]
    another operation x12 -> x13, local copies, waits for them, and re-layouts: 10.8 us -> 12.4 us
where the time goes in v1:
time: 340 us; the launch traced here: 335 us
  other arithmetic  128 us (38%)
  blocking collectives  66.6 us (20%)
  starting transfers between devices  41.6 us (12%)
  local copies, waits for them, and re-layouts  36.5 us (11%)
  between operations  21.9 us (6%)
  waiting for transfers between devices  19.8 us (6%)
  matrix products  19.7 us (6%)
    another operation x14, other arithmetic, shards(): factor = jnp.linalg.cholesky(gram_matrix)  78.6 us
    all_gather x3, blocking collectives, gather_in_order(): tiles = lax.all_gather(tiles, axes[k], axis=0, tiled=True)  42.7 us
    another operation x3, other arithmetic, shards(): inverse = jax.scipy.linalg.cho_solve((factor, True), pivot_block.T)  40.3 us
    all_gather x1, blocking collectives, shards(): lax.all_gather(whole_pivot.astype(jnp.bfloat16), 'sub', axis=0, tiled=True)  24 us
    all_to_all x1, waiting for transfers between devices, shards(): partner = jnp.concatenate(lax.all_to_all(outgoing, 'sub', 0, 0), axis=1)  19.7 us
    all_to_all x1, starting transfers between devices, shards(): lax.all_to_all(pivot_part.astype(jnp.bfloat16), TRI, split_axis=0, concat...  19.3 us
    all_to_all x1, starting transfers between devices, shards(): lax.all_to_all(holder_part.reshape(tri_count, piece_size), TRI, split_axi...  14.6 us
    another operation x12, local copies, waits for them, and re-layouts  10.9 us
  transfers between devices with their start and end apart: 4, of which 1 were waited for; matrix products, arithmetic and copies ran while one was open for 48% of the time, Pallas kernels for 0%

profile of v1, /device:TPU:1, one launch (start us, length us, event | category | flops | bytes accessed | tf_op | source)
XLA Modules:
  0.0 334.6 jit_solution(18107565832825047004)
XLA Ops:
  11.3 19.3 %all-to-all-start.1 = ((bf16[64,2,256]{2,1,0:T(2,128)(2,1)}), bf16[64,2,256]{2,1,0:T(2,128)(2,1)S(1)}, u32[]{:S(2)}, u32[]{:S(2)}) async-start(bf16[64,2,256]{2,1,0:T(2,128)(2,1)} %reshape.313), calls=%async_computation.1 | async-start | bytes 131072 | tf_op jit(solution)/shard_map/all_to_all | solution.py:99
  43.1 2.1 reduce.26
  46.2 14.6 %all-to-all-start = ((bf16[64,2,1024]{2,1,0:T(2,128)(2,1)}), bf16[64,2,1024]{2,1,0:T(2,128)(2,1)S(1)}, u32[]{:S(2)}, u32[]{:S(2)}) async-start(bf16[64,2,1024]{2,1,0:T(2,128)(2,1)} %reshape.315), calls=%async_computation | async-start | bytes 524288 | tf_op jit(solution)/shard_map/all_to_all | solution.py:96
  60.9 8.8 %all_gather.17 = bf16[4,1,512]{2,1,0:T(2,128)(2,1)S(1)} all-gather(bf16[1,1,512]{2,1,0:T(2,128)(2,1)S(1)} %fusion.54), channel_id=1, replica_groups=mesh['tri_0'=4,'tri_1'=16,'sub'=8] {'tri_0'}, dimensions={0}, use_global_device_ids=true | all-gather | bytes 5120 | tf_op jit(solution)/shard_map/all_gather | solution.py:22
  69.7 23.8 %all_gather.18 = bf16[64,1,512]{2,1,0:T(2,128)(2,1)S(1)} all-gather(bf16[4,1,512]{2,1,0:T(2,128)(2,1)S(1)} %all_gather.17), channel_id=1, replica_groups=mesh['tri_0'=4,'tri_1'=16,'sub'=8] {'tri_1'}, dimensions={0}, use_global_device_ids=true | all-gather | bytes 69632 | tf_op jit(solution)/shard_map/all_gather | solution.py:22
  93.9 24.0 %all_gather.19 = bf16[512,512]{1,0:T(8,128)(2,1)S(1)} all-gather(bf16[64,512]{1,0:T(8,128)(2,1)S(1)} %bitcast.124), channel_id=1, replica_groups=mesh['tri_0'=4,'tri_1'=16,'sub'=8] {'sub'}, dimensions={0}, use_global_device_ids=true | all-gather | bytes 589824 | tf_op jit(solution)/shard_map/all_gather | solution.py:111
  120.7 11.7 %cholesky.104 = f32[128,128]{1,0:T(8,128)S(1)} custom-call(f32[128,128]{1,0:T(8,128)S(1)} %cholesky.266), custom_call_target="Cholesky" | custom-call | tf_op jit(solution)/shard_map/jit(cholesky)/cholesky | solution.py:117
  132.4 9.8 %custom-call.34 = f32[1,128,128]{1,2,0:T(8,128)S(1)} custom-call(f32[1,128,128]{2,1,0:T(8,128)S(1)} %get-tuple-element.32), custom_call_target="InvertDiagBlocksLowerTriangular" | custom-call | tf_op jit(solution)/shard_map/jit(cholesky)/cholesky | solution.py:117
  144.9 11.7 %cholesky.217 = f32[128,128]{1,0:T(8,128)S(1)} custom-call(f32[128,128]{1,0:T(8,128)S(1)} %cholesky.270), custom_call_target="Cholesky" | custom-call | tf_op jit(solution)/shard_map/jit(cholesky)/cholesky | solution.py:117
  156.7 10.0 %custom-call.35 = f32[1,128,128]{1,2,0:T(8,128)S(1)} custom-call(f32[1,128,128]{2,1,0:T(8,128)S(1)} %get-tuple-element.29), custom_call_target="InvertDiagBlocksLowerTriangular" | custom-call | tf_op jit(solution)/shard_map/jit(cholesky)/cholesky | solution.py:117
  168.2 11.7 %cholesky.238 = f32[128,128]{1,0:T(8,128)S(1)} custom-call(f32[128,128]{1,0:T(8,128)S(1)} %cholesky.275), custom_call_target="Cholesky" | custom-call | tf_op jit(solution)/shard_map/jit(cholesky)/cholesky | solution.py:117
  179.9 9.8 %custom-call.36 = f32[1,128,128]{1,2,0:T(8,128)S(1)} custom-call(f32[1,128,128]{2,1,0:T(8,128)S(1)} %get-tuple-element.26), custom_call_target="InvertDiagBlocksLowerTriangular" | custom-call | tf_op jit(solution)/shard_map/jit(cholesky)/cholesky | solution.py:117
  191.0 10.1 %all-gather = bf16[32,2048]{1,0:T(8,128)(2,1)} all-gather(bf16[8,2048]{1,0:T(8,128)(2,1)S(1)} %gather_fusion.3), channel_id=2, replica_groups=mesh['tri_0'=4,'tri_1'=16,'sub'=8] {'tri_0'}, dimensions={0}, use_global_device_ids=true | all-gather | bytes 163840 | tf_op jit(solution)/shard_map/all_gather | solution.py:22
  202.5 11.7 %cholesky.255 = f32[128,128]{1,0:T(8,128)S(1)} custom-call(f32[128,128]{1,0:T(8,128)S(1)} %convolution_subtract_fusion.8), custom_call_target="Cholesky" | custom-call | tf_op jit(solution)/shard_map/jit(cholesky)/cholesky | solution.py:117
  219.0 10.9 %while.1 = (s32[]{:T(128)}, f32[512,512]{1,0:T(8,128)S(1)}, s32[4,2]{0,1:T(2,128)S(1)}, f32[4,128,128]{2,1,0:T(8,128)}, s32[]{:T(128)}) while((s32[]{:T(128)}, f32[512,512]{1,0:T(8,128)S(1)}, s32[4,2]{0,1:T(2,128)S(1)}, f32[4,128,128]{2,1,0:T(8,128)}, s32[]{:T(128)}) %tuple.27), condition=%wide.while_cond, body=%wide.while_body.sunk | while | flops 2 | bytes 132205 | solution.py:118
  219.7 2.0 bitcast_dynamic-update-slice_fusion.2
  225.2 2.0 bitcast_dynamic-update-slice_fusion.2
  227.9 2.0 bitcast_dynamic-update-slice_fusion.2
  229.9 40.1 %custom-call.37 = f32[4,128,128]{1,2,0:T(8,128)S(1)} custom-call(f32[4,128,128]{2,1,0:T(8,128)} %get-tuple-element.12), custom_call_target="InvertDiagBlocksLowerTriangular" | custom-call | tf_op jit(solution)/shard_map/jit(_cho_solve)/triangular_solve | solution.py:118
  277.2 2.6 reshape_reshape.6
  282.3 7.7 %all-to-all-start.2 = ((bf16[8,4,64,512]{3,2,1,0:T(8,128)(2,1)}), bf16[8,4,64,512]{3,2,1,0:T(8,128)(2,1)}, u32[]{:S(2)}, u32[]{:S(2)}) async-start(bf16[8,4,64,512]{3,2,1,0:T(8,128)(2,1)} %stack.3), calls=%async_computation.2 | async-start | bytes 4194304 | tf_op jit(solution)/shard_map/all_to_all | solution.py:115
  296.6 19.7 %all-to-all-done.2 = bf16[8,4,64,512]{3,2,1,0:T(8,128)(2,1)} async-done(((bf16[8,4,64,512]{3,2,1,0:T(8,128)(2,1)}), bf16[8,4,64,512]{3,2,1,0:T(8,128)(2,1)}, u32[]{:S(2)}, u32[]{:S(2)}) %all-to-all-start.2) | async-done | bytes 2097184 | tf_op jit(solution)/shard_map/all_to_all | solution.py:115
  318.2 3.9 %gather_fusion.5 = bf16[10,512,512]{2,1,0:T(8,128)(2,1)} fusion(bf16[4,512,512]{2,1,0:T(8,128)(2,1)S(1)} %bitcast.116, s32[1024]{0:T(1024)S(1)} %pad_clamp_fusion), kind=kCustom, calls=%fused_computation.5 | custom fusion | bytes 10485800 | tf_op jit(solution)/shard_map/gather | solution.py:123
  322.0 5.4 %fusion.1 = f32[1,10,64,512]{3,2,1,0:T(8,128)} fusion(bf16[10,64,512]{2,1,0:T(8,128)(2,1)} %gather_fusion.4, bf16[10,512,512]{2,1,0:T(8,128)(2,1)} %gather_fusion.5, pred[10]{0:T(512)(128)(4,1)S(1)} %and_bitcast_fusion, f32[1,10,64,512]{3,2,1,0:T(8,128)S(1)} %copy-done.2), kind=kOutput, calls=%fused_computation.10 | convolution fusion | flops 336199680 | bytes 8519690 | tf_op jit(solution)/shard_map/qrk,qck->qrc/dot_general | solution.py:124
  (110 shorter events, 48.1 us)
Async XLA Ops:
  6.5 35.5 %copy-start.8 = (f32[4]{0:T(128)S(1)}, f32[4]{0:T(128)}, u32[]{:S(2)}) copy-start(f32[4]{0:T(128)} %constant.245) | copy-start | bytes 52
  11.3 34.9 %all-to-all-start.1 = ((bf16[64,2,256]{2,1,0:T(2,128)(2,1)}), bf16[64,2,256]{2,1,0:T(2,128)(2,1)S(1)}, u32[]{:S(2)}, u32[]{:S(2)}) async-start(bf16[64,2,256]{2,1,0:T(2,128)(2,1)} %reshape.313), calls=%async_computation.1 | async-start | bytes 131072 | tf_op jit(solution)/shard_map/all_to_all | solution.py:99
  46.2 143.8 %all-to-all-start = ((bf16[64,2,1024]{2,1,0:T(2,128)(2,1)}), bf16[64,2,1024]{2,1,0:T(2,128)(2,1)S(1)}, u32[]{:S(2)}, u32[]{:S(2)}) async-start(bf16[64,2,1024]{2,1,0:T(2,128)(2,1)} %reshape.315), calls=%async_computation | async-start | bytes 524288 | tf_op jit(solution)/shard_map/all_to_all | solution.py:96
  60.7 213.5 %all-gather.3.cloned.1.call-start = ((), (), s32[]{:S(2)}) async-start(), calls=%async_computation.3 | async-start | bytes 2228224 | tf_op jit(solution)/shard_map/all_gather | solution.py:22
  270.1 1.7 copy-start.5
  271.3 0.9 copy-start
  272.2 0.7 copy-start.3
  282.3 7.7 %copy-start.6 = (f32[4,128,128]{1,2,0:T(8,128)S(1)}, f32[4,128,128]{1,2,0:T(8,128)}, u32[]{:S(2)}) copy-start(f32[4,128,128]{1,2,0:T(8,128)} %copy-done.5) | copy-start | bytes 786436
  282.3 7.7 %copy-start.7 = (f32[128,512]{1,0:T(8,128)S(1)}, f32[128,512]{1,0:T(8,128)}, u32[]{:S(2)}) copy-start(f32[128,512]{1,0:T(8,128)} %convolution_subtract_fusion.5) | copy-start | bytes 786436
  282.3 8.5 %copy-start.4 = (f32[128,512]{1,0:T(8,128)S(1)}, f32[128,512]{1,0:T(8,128)}, u32[]{:S(2)}) copy-start(f32[128,512]{1,0:T(8,128)} %copy-done.3) | copy-start | bytes 786436
  282.3 34.1 %all-to-all-start.2 = ((bf16[8,4,64,512]{3,2,1,0:T(8,128)(2,1)}), bf16[8,4,64,512]{3,2,1,0:T(8,128)(2,1)}, u32[]{:S(2)}, u32[]{:S(2)}) async-start(bf16[8,4,64,512]{3,2,1,0:T(8,128)(2,1)} %stack.3), calls=%async_computation.2 | async-start | bytes 4194304 | tf_op jit(solution)/shard_map/all_to_all | solution.py:115
  290.0 1.6 copy-start.1
  318.1 3.9 %copy-start.2 = (f32[1,10,64,512]{3,2,1,0:T(8,128)S(1)}, f32[1,10,64,512]{3,2,1,0:T(8,128)}, u32[]{:S(2)}) copy-start(f32[1,10,64,512]{3,2,1,0:T(8,128)} %param.9) | copy-start | bytes 3932164
Sparse Core Ops, SparseCore 0:
  201.2 63.6 all-gather.2
